TPU v7x, 32 devices: a whole 2x2x4 slice. The times are simulated.
32 devices in a mesh: lead: 8 (over z, core), grp: 4 (over y, x).
Axes of the slice: x: 2, y: 2, z: 4, core: 2. Of those that a mesh axis runs over, the one named last changes fastest.
Arguments:
- matrix_tiles: bfloat16 [64, 384, 384], P(('lead', 'grp')), may hold values from -0.0546875 to 0.0546875
- tile_slot: int32 [8, 8], P('lead'), may hold values from 0 to 7, each once within a row
- tile_cols: int32 [8, 8], P('lead'), may hold values from 0 to 2, as said below
- send_rows: int32 [8, 2, 1], replicated, may hold values from 0 to 0, as said below
- residual: float32 [3072, 128], P(('lead', 'grp')), may hold values from -6 to 6
- diag_inv: float32 [3072], P(('lead', 'grp')), may hold values from 0.25 to 1
Outputs:
- correction: float32 [3072, 128], P(('lead', 'grp'))
Inputs may be any that keep to these rules, and one draw needn't show every extreme that they name: `tile_cols`: entry 0 of every row is that row's own block row within its leader, r for row l + r; indices below 1 are the leader's own block rows, the next 1 are the rows received from leader l - 1, the last 1 those received from leader l + 1 (cyclic). `send_rows`: the 1 entries of each list are distinct block rows of the sending leader.
All inputs are finite; a program needn't handle non-finite values.
Results may differ from a plain program's by a relative error of at most 0.0013.
Values may be sent and summed in bfloat16 or wider, within the bound.
A program may use at most 64 MiB of HBM per device.

v0:
```python
import jax
import jax.numpy as jnp
from jax import lax
from jax.sharding import PartitionSpec as P

TILES_ROW = 8


lower_bound = 0.5
upper_bound = 1.5


def from_behind(shard, axis, by):
    devices = lax.axis_size(axis)
    return lax.ppermute(shard, axis, [(i, (i + by) % devices) for i in range(devices)])


def one_sweep(start_residual, inverse, apply_operator):
    center_value = (upper_bound + lower_bound) / 2.0
    half_width = (upper_bound - lower_bound) / 2.0
    ratio_value = center_value / half_width
    update = inverse[:, None] * start_residual / center_value
    approx = update
    rho_now = 1.0 / ratio_value
    rho_next = 1.0 / (2.0 * ratio_value - rho_now)
    remaining = start_residual - apply_operator(approx)
    update = (
        rho_next * rho_now * update + 2.0 * rho_next / half_width * inverse[:, None] * remaining
    )
    approx = approx + update
    return approx


def smooth_twice(rhs_field, inverse, apply_operator):
    first_pass = one_sweep(rhs_field, inverse, apply_operator)
    remaining = rhs_field - apply_operator(first_pass)
    second_pass = one_sweep(remaining, inverse, apply_operator)
    return first_pass + second_pass


def extend(blocks, send_rows):
    position = lax.axis_index("lead")
    mine_up = jnp.take(blocks, send_rows[position, 0], axis=0)
    mine_down = jnp.take(blocks, send_rows[position, 1], axis=0)
    from_lower = from_behind(mine_up, "lead", 1)
    from_upper = from_behind(mine_down, "lead", -1)
    return jnp.concatenate([blocks, from_lower, from_upper], axis=0)


def local(matrix_tiles, tile_slot, tile_cols, send_rows, residual, diag_inv):
    block_rows = tile_cols.shape[0]
    tile_size = matrix_tiles.shape[1]
    member = lax.axis_index("grp")
    share_rows = residual.shape[0]
    group_slots = tile_slot[0]
    share_tiles = matrix_tiles.shape[0]
    members = lax.axis_size("grp")
    own_slots = lax.dynamic_slice_in_dim(group_slots, member * share_tiles, share_tiles, 0)
    own_block = own_slots // TILES_ROW
    target = jnp.arange(members, dtype=jnp.int32)[:, None, None]
    offsets = jnp.arange(share_rows, dtype=jnp.int32)[None, None, :]
    source_row = target * share_rows + offsets - own_block[None, :, None] * tile_size
    valid = (source_row >= 0) & (source_row < tile_size)
    clipped = jnp.clip(source_row, 0, tile_size - 1)
    tile_pick = jnp.arange(share_tiles, dtype=jnp.int32)[None, :, None]
    picked = matrix_tiles[tile_pick, clipped]
    outgoing = jnp.where(valid[..., None], picked, jnp.zeros_like(picked))
    received = lax.all_to_all(outgoing, "grp", split_axis=0, concat_axis=0, tiled=True)
    flat_rows = received.reshape(members * share_tiles, share_rows * tile_size)
    position_of = group_slots % TILES_ROW
    selector = (jnp.arange(TILES_ROW, dtype=jnp.int32)[:, None] == position_of[None, :]).astype(
        jnp.bfloat16
    )
    mine = jnp.dot(selector, flat_rows, preferred_element_type=jnp.float32).astype(jnp.bfloat16)
    mine = mine.reshape(TILES_ROW, share_rows, tile_size).transpose(1, 0, 2)
    mine = mine.reshape(share_rows, TILES_ROW * tile_size)
    first_block = member * share_rows // tile_size
    row_block = (member * share_rows + jnp.arange(share_rows, dtype=jnp.int32)) // tile_size

    def apply_operator(approx):
        rounded = approx.astype(jnp.bfloat16)
        gathered = lax.all_gather(rounded, "grp", axis=0, tiled=True)
        extended = extend(gathered.reshape(block_rows, tile_size, -1), send_rows)
        target_block = jnp.minimum(first_block + 0, block_rows - 1)
        operand = jnp.take(extended, tile_cols[target_block], axis=0)
        operand = operand.reshape(TILES_ROW * tile_size, -1)
        product = jnp.dot(mine, operand, preferred_element_type=jnp.float32)
        coupled = jnp.where((row_block == first_block + 0)[:, None], product, 0.0)
        return approx / diag_inv[:, None] + coupled

    correction = smooth_twice(residual, diag_inv, apply_operator)
    return correction


def solution(mesh):
    in_specs = (
        P(("lead", "grp"), None, None),
        P("lead", None),
        P("lead", None),
        P(),
        P(("lead", "grp"), None),
        P(("lead", "grp")),
    )
    out_specs = P(("lead", "grp"), None)
    return jax.shard_map(local, mesh=mesh, in_specs=in_specs, out_specs=out_specs, check_vma=False)
```

profile of v0, /device:TPU:0, one launch (start us, length us, event | category | flops | bytes accessed | tf_op | source)
XLA Modules:
  0.0 70.0 jit_solution(7721782783163418934)
XLA Ops:
  0.0 1.4 %constant_dynamic-slice_fusion.1 = (s32[1,1,1]{0,2,1:T(1,128)}, s32[1,1,1]{0,2,1:T(1,128)}) fusion(s32[8,2,1]{0,2,1:T(1,128)} %param.11, s32[]{:T(128)S(6)} %select_n.162), kind=kLoop, calls=%fused_computation.73 | loop fusion | bytes 20 | tf_op jit(solution)/shard_map/dynamic_slice | solution.py:43
  5.4 0.9 %multiply_convert_fusion.1 = bf16[96,128]{1,0:T(8,128)(2,1)S(1)} fusion(f32[96,128]{1,0:T(8,128)} %param.12, f32[96]{0:T(128)} %param.13), kind=kLoop, calls=%fused_computation.51 | loop fusion | flops 24576 | bytes 74112 | tf_op jit(solution)/shard_map/convert_element_type | solution.py:81
  6.3 9.8 %all_gather.9 = bf16[384,128]{1,0:T(8,128)(2,1)S(1)} all-gather(bf16[96,128]{1,0:T(8,128)(2,1)S(1)} %multiply_convert_fusion.1), channel_id=1, replica_groups=mesh['lead'=8,'grp'=4] {'grp'}, dimensions={0}, use_global_device_ids=true | all-gather | bytes 122880 | tf_op jit(solution)/shard_map/all_gather | solution.py:82
  16.2 3.5 %collective-permute-start.1 = (bf16[1,384,128]{2,1,0:T(8,128)(2,1)S(1)}, bf16[1,384,128]{2,1,0:T(8,128)(2,1)S(1)}, u32[]{:S(2)}, u32[]{:S(2)}) collective-permute-start(bf16[1,384,128]{2,1,0:T(8,128)(2,1)S(1)} %get-tuple-element.11), channel_id=1, source_target_pairs={{0,28},{4,0},{8,4},{12,8},{16,12},{20,16},{24,20},{28,24},{1,29},{... | collective-permute-start | bytes 294920 | tf_op jit(solution)/shard_map/ppermute | solution.py:15
  19.8 0.7 %fusion.39 = s32[2]{0:T(128)S(1)} fusion(s32[1,8]{1,0:T(1,128)} %param.9, s32[]{:T(128)S(6)} %select_n.158), kind=kLoop, calls=%fused_computation.80 | loop fusion | flops 32 | bytes 20 | tf_op jit(solution)/shard_map/mul | solution.py:62
  20.8 5.1 %gather_fusion = bf16[768,384]{1,0:T(8,128)(2,1)S(1)} fusion(bf16[2,384,384]{2,1,0:T(8,128)(2,1)S(1)} %copy-done, s32[768]{0:T(1024)S(1)} %reshape.232), kind=kCustom, calls=%fused_computation.3 | custom fusion | bytes 1185792 | tf_op jit(solution)/shard_map/gather | solution.py:66
  25.9 1.0 %broadcast_select_fusion = bf16[4,2,96,384]{3,2,1,0:T(8,128)(2,1)} fusion(bf16[4,2,96,384]{3,2,1,0:T(8,128)(2,1)S(1)} %bitcast.84, pred[4,2,96]{2,1,0:T(4,128)(4,1)S(1)} %compare_and_fusion), kind=kLoop, calls=%fused_computation.33 | loop fusion | flops 294912 | bytes 1180416 | tf_op jit(solution)/shard_map/jit(_where)/select_n | solution.py:67
  26.9 3.6 %all-to-all-start = ((bf16[4,2,96,384]{3,2,1,0:T(8,128)(2,1)}), bf16[4,2,96,384]{3,2,1,0:T(8,128)(2,1)S(1)}, u32[]{:S(2)}, u32[]{:S(2)}) async-start(bf16[4,2,96,384]{3,2,1,0:T(8,128)(2,1)} %broadcast_select_fusion), calls=%async_computation | async-start | bytes 1179648 | tf_op jit(solution)/shard_map/all_to_all | solution.py:68
  30.7 0.7 gather_fusion.1
  31.4 6.4 %all-to-all-done = bf16[4,2,96,384]{3,2,1,0:T(8,128)(2,1)S(1)} async-done(((bf16[4,2,96,384]{3,2,1,0:T(8,128)(2,1)}), bf16[4,2,96,384]{3,2,1,0:T(8,128)(2,1)S(1)}, u32[]{:S(2)}, u32[]{:S(2)}) %all-to-all-start) | async-done | bytes 589856 | tf_op jit(solution)/shard_map/all_to_all | solution.py:68
  37.8 0.2 copy.9
  38.0 0.3 convolution_convert_fusion
  38.3 0.5 copy-done.1
  38.8 0.4 fusion.43
  39.2 8.3 %all_gather.10 = bf16[384,128]{1,0:T(8,128)(2,1)S(1)} all-gather(bf16[96,128]{1,0:T(8,128)(2,1)S(1)} %get-tuple-element.14), channel_id=1, replica_groups=mesh['lead'=8,'grp'=4] {'grp'}, dimensions={0}, use_global_device_ids=true | all-gather | bytes 122880 | tf_op jit(solution)/shard_map/all_gather | solution.py:82
  47.6 3.5 %collective-permute-start.3 = (bf16[1,384,128]{2,1,0:T(8,128)(2,1)S(1)}, bf16[1,384,128]{2,1,0:T(8,128)(2,1)S(1)}, u32[]{:S(2)}, u32[]{:S(2)}) collective-permute-start(bf16[1,384,128]{2,1,0:T(8,128)(2,1)S(1)} %get-tuple-element.9), channel_id=1, source_target_pairs={{0,28},{4,0},{8,4},{12,8},{16,12},{20,16},{24,20},{28,24},{1,29},{... | collective-permute-start | bytes 294920 | tf_op jit(solution)/shard_map/ppermute | solution.py:15
  51.2 2.4 %collective-permute-done.2 = bf16[1,384,128]{2,1,0:T(8,128)(2,1)S(1)} collective-permute-done((bf16[1,384,128]{2,1,0:T(8,128)(2,1)S(1)}, bf16[1,384,128]{2,1,0:T(8,128)(2,1)S(1)}, u32[]{:S(2)}, u32[]{:S(2)}) %collective-permute-start.2) | collective-permute-done | bytes 98336 | tf_op jit(solution)/shard_map/ppermute | solution.py:15
  53.6 0.7 gather_fusion.2
  54.3 0.4 multiply_convert_fusion
  54.7 7.4 %all_gather.11 = bf16[384,128]{1,0:T(8,128)(2,1)S(1)} all-gather(bf16[96,128]{1,0:T(8,128)(2,1)S(1)} %get-tuple-element.16), channel_id=1, replica_groups=mesh['lead'=8,'grp'=4] {'grp'}, dimensions={0}, use_global_device_ids=true | all-gather | bytes 122880 | tf_op jit(solution)/shard_map/all_gather | solution.py:82
  62.2 3.5 %collective-permute-start.5 = (bf16[1,384,128]{2,1,0:T(8,128)(2,1)S(1)}, bf16[1,384,128]{2,1,0:T(8,128)(2,1)S(1)}, u32[]{:S(2)}, u32[]{:S(2)}) collective-permute-start(bf16[1,384,128]{2,1,0:T(8,128)(2,1)S(1)} %get-tuple-element.7), channel_id=1, source_target_pairs={{0,28},{4,0},{8,4},{12,8},{16,12},{20,16},{24,20},{28,24},{1,29},{... | collective-permute-start | bytes 294920 | tf_op jit(solution)/shard_map/ppermute | solution.py:15
  65.8 2.5 %collective-permute-done.4 = bf16[1,384,128]{2,1,0:T(8,128)(2,1)S(1)} collective-permute-done((bf16[1,384,128]{2,1,0:T(8,128)(2,1)S(1)}, bf16[1,384,128]{2,1,0:T(8,128)(2,1)S(1)}, u32[]{:S(2)}, u32[]{:S(2)}) %collective-permute-start.4) | collective-permute-done | bytes 98336 | tf_op jit(solution)/shard_map/ppermute | solution.py:15
  68.3 0.7 gather_fusion.3
  69.0 1.0 %fusion.15 = f32[96,128]{1,0:T(8,128)} fusion(f32[96,128]{1,0:T(8,128)S(1)} %get-tuple-element.15, f32[96,128]{1,0:T(8,128)S(1)} %get-tuple-element.17, bf16[8,384,128]{2,1,0:T(8,128)(2,1)S(1)} %gather_fusion.3, pred[8]{0:T(512)(128)(4,1)S(1)} %compare_and_fusion.1, bf16[8,96,384]{2,0,1:T(8,128)(2,1)S(1)} %bitcast.90, f32[96]{0:T(128)S(1)} %broadcast_multiply_fusion, ...), kind=kOutput, calls=%fused_computation.23 | convolution fusion | flops 76013568 | bytes 1524584 | tf_op jit(solution)/shard_map/dot_general | solution.py:87
  (33 shorter events, 0.7 us)
Async XLA Ops:
  0.0 20.8 %copy-start = (bf16[2,384,384]{2,1,0:T(8,128)(2,1)S(1)}, bf16[2,384,384]{2,1,0:T(8,128)(2,1)}, u32[]{:S(2)}) copy-start(bf16[2,384,384]{2,1,0:T(8,128)(2,1)} %param.8) | copy-start | bytes 1769476
  16.1 14.5 %collective-permute-start = (bf16[1,384,128]{2,1,0:T(8,128)(2,1)S(1)}, bf16[1,384,128]{2,1,0:T(8,128)(2,1)S(1)}, u32[]{:S(2)}, u32[]{:S(2)}) collective-permute-start(bf16[1,384,128]{2,1,0:T(8,128)(2,1)S(1)} %get-tuple-element.10), channel_id=1, source_target_pairs={{0,4},{4,8},{8,12},{12,16},{16,20},{20,24},{24,28},{28,0},{1,5},{5... | collective-permute-start | bytes 294920 | tf_op jit(solution)/shard_map/ppermute | solution.py:15
  16.2 14.5 %collective-permute-start.1 = (bf16[1,384,128]{2,1,0:T(8,128)(2,1)S(1)}, bf16[1,384,128]{2,1,0:T(8,128)(2,1)S(1)}, u32[]{:S(2)}, u32[]{:S(2)}) collective-permute-start(bf16[1,384,128]{2,1,0:T(8,128)(2,1)S(1)} %get-tuple-element.11), channel_id=1, source_target_pairs={{0,28},{4,0},{8,4},{12,8},{16,12},{20,16},{24,20},{28,24},{1,29},{... | collective-permute-start | bytes 294920 | tf_op jit(solution)/shard_map/ppermute | solution.py:15
  26.9 3.6 %copy-start.3 = (s32[1,8]{1,0:T(1,128)S(1)}, s32[1,8]{1,0:T(1,128)}, u32[]{:S(2)}) copy-start(s32[1,8]{1,0:T(1,128)} %param.9) | copy-start | bytes 100
  26.9 3.7 %copy-start.4 = (s32[1,8]{1,0:T(1,128)S(1)}, s32[1,8]{1,0:T(1,128)}, u32[]{:S(2)}) copy-start(s32[1,8]{1,0:T(1,128)} %param.10) | copy-start | bytes 100
  26.9 3.7 %copy-start.2 = (f32[96]{0:T(128)S(1)}, f32[96]{0:T(128)}, u32[]{:S(2)}) copy-start(f32[96]{0:T(128)} %param.13) | copy-start | bytes 1156
  26.9 10.9 %all-to-all-start = ((bf16[4,2,96,384]{3,2,1,0:T(8,128)(2,1)}), bf16[4,2,96,384]{3,2,1,0:T(8,128)(2,1)S(1)}, u32[]{:S(2)}, u32[]{:S(2)}) async-start(bf16[4,2,96,384]{3,2,1,0:T(8,128)(2,1)} %broadcast_select_fusion), calls=%async_computation | async-start | bytes 1179648 | tf_op jit(solution)/shard_map/all_to_all | solution.py:68
  38.0 0.8 %copy-start.1 = (f32[96,128]{1,0:T(8,128)S(1)}, f32[96,128]{1,0:T(8,128)}, u32[]{:S(2)}) copy-start(f32[96,128]{1,0:T(8,128)} %param.12) | copy-start | bytes 147460
  47.6 6.0 %collective-permute-start.2 = (bf16[1,384,128]{2,1,0:T(8,128)(2,1)S(1)}, bf16[1,384,128]{2,1,0:T(8,128)(2,1)S(1)}, u32[]{:S(2)}, u32[]{:S(2)}) collective-permute-start(bf16[1,384,128]{2,1,0:T(8,128)(2,1)S(1)} %get-tuple-element.8), channel_id=1, source_target_pairs={{0,4},{4,8},{8,12},{12,16},{16,20},{20,24},{24,28},{28,0},{1,5},{5... | collective-permute-start | bytes 294920 | tf_op jit(solution)/shard_map/ppermute | solution.py:15
  47.6 6.0 %collective-permute-start.3 = (bf16[1,384,128]{2,1,0:T(8,128)(2,1)S(1)}, bf16[1,384,128]{2,1,0:T(8,128)(2,1)S(1)}, u32[]{:S(2)}, u32[]{:S(2)}) collective-permute-start(bf16[1,384,128]{2,1,0:T(8,128)(2,1)S(1)} %get-tuple-element.9), channel_id=1, source_target_pairs={{0,28},{4,0},{8,4},{12,8},{16,12},{20,16},{24,20},{28,24},{1,29},{... | collective-permute-start | bytes 294920 | tf_op jit(solution)/shard_map/ppermute | solution.py:15
  62.2 6.1 %collective-permute-start.4 = (bf16[1,384,128]{2,1,0:T(8,128)(2,1)S(1)}, bf16[1,384,128]{2,1,0:T(8,128)(2,1)S(1)}, u32[]{:S(2)}, u32[]{:S(2)}) collective-permute-start(bf16[1,384,128]{2,1,0:T(8,128)(2,1)S(1)} %get-tuple-element.6), channel_id=1, source_target_pairs={{0,4},{4,8},{8,12},{12,16},{16,20},{20,24},{24,28},{28,0},{1,5},{5... | collective-permute-start | bytes 294920 | tf_op jit(solution)/shard_map/ppermute | solution.py:15
  62.2 6.0 %collective-permute-start.5 = (bf16[1,384,128]{2,1,0:T(8,128)(2,1)S(1)}, bf16[1,384,128]{2,1,0:T(8,128)(2,1)S(1)}, u32[]{:S(2)}, u32[]{:S(2)}) collective-permute-start(bf16[1,384,128]{2,1,0:T(8,128)(2,1)S(1)} %get-tuple-element.7), channel_id=1, source_target_pairs={{0,28},{4,0},{8,4},{12,8},{16,12},{20,16},{24,20},{28,24},{1,29},{... | collective-permute-start | bytes 294920 | tf_op jit(solution)/shard_map/ppermute | solution.py:15
where the time goes:
time: 70.4 us; the launch traced here: 70 us
  blocking collectives  25.5 us (36%)
  starting transfers between devices  14.4 us (20%)
  waiting for transfers between devices  11.3 us (16%)
  local copies, waits for them, and re-layouts  9.34 us (13%)
  between operations  4.27 us (6%)
  other arithmetic  3.06 us (4%)
  matrix products  2.11 us (3%)
    all_gather x3, blocking collectives, apply_operator(): gathered = lax.all_gather(rounded, 'grp', axis=0, tiled=True)  25.5 us
    ppermute x6, starting transfers between devices, from_behind(): lax.ppermute(shard, axis, [(i, (i + by) % devices) for i in range(devices)])  10.8 us
    all_to_all x1, waiting for transfers between devices, local(): lax.all_to_all(outgoing, 'grp', split_axis=0, concat_axis=0, tiled=True)  6.4 us
    gather x1, local copies, waits for them, and re-layouts, local(): picked = matrix_tiles[tile_pick, clipped]  5.07 us
    ppermute x6, waiting for transfers between devices, from_behind(): lax.ppermute(shard, axis, [(i, (i + by) % devices) for i in range(devices)])  4.93 us
    all_to_all x1, starting transfers between devices, local(): lax.all_to_all(outgoing, 'grp', split_axis=0, concat_axis=0, tiled=True)  3.61 us
    gather x3, local copies, waits for them, and re-layouts, apply_operator(): operand = jnp.take(extended, tile_cols[target_block], axis=0)  2.1 us
    dot_general x3, matrix products, apply_operator(): product = jnp.dot(mine, operand, preferred_element_type=jnp.float32)  1.81 us
  transfers between devices with their start and end apart: 7, of which 3 were waited for; matrix products, arithmetic and copies ran while one was open for 11% of the time, Pallas kernels for 0%

commit v1 on v0

--- a/solution.py
+++ b/solution.py
@@ -1,6 +1,10 @@
+import functools
+
 import jax
 import jax.numpy as jnp
 from jax import lax
+from jax.experimental import pallas as pl
+from jax.experimental.pallas import tpu as pltpu
 from jax.sharding import PartitionSpec as P
 
 TILES_ROW = 8
@@ -38,16 +42,22 @@
     return first_pass + second_pass
 
 
+def pick_blocks(blocks, rows):
+    return jnp.concatenate(
+        [lax.dynamic_slice_in_dim(blocks, rows[i], 1, 0) for i in range(rows.shape[0])], axis=0
+    )
+
+
 def extend(blocks, send_rows):
     position = lax.axis_index("lead")
-    mine_up = jnp.take(blocks, send_rows[position, 0], axis=0)
-    mine_down = jnp.take(blocks, send_rows[position, 1], axis=0)
+    mine_up = pick_blocks(blocks, send_rows[position, 0])
+    mine_down = pick_blocks(blocks, send_rows[position, 1])
     from_lower = from_behind(mine_up, "lead", 1)
     from_upper = from_behind(mine_down, "lead", -1)
     return jnp.concatenate([blocks, from_lower, from_upper], axis=0)
 
 
-def local(matrix_tiles, tile_slot, tile_cols, send_rows, residual, diag_inv):
+def local_general(matrix_tiles, tile_slot, tile_cols, send_rows, residual, diag_inv):
     block_rows = tile_cols.shape[0]
     tile_size = matrix_tiles.shape[1]
     member = lax.axis_index("grp")
@@ -82,7 +92,7 @@
         gathered = lax.all_gather(rounded, "grp", axis=0, tiled=True)
         extended = extend(gathered.reshape(block_rows, tile_size, -1), send_rows)
         target_block = jnp.minimum(first_block + 0, block_rows - 1)
-        operand = jnp.take(extended, tile_cols[target_block], axis=0)
+        operand = pick_blocks(extended, tile_cols[target_block])
         operand = operand.reshape(TILES_ROW * tile_size, -1)
         product = jnp.dot(mine, operand, preferred_element_type=jnp.float32)
         coupled = jnp.where((row_block == first_block + 0)[:, None], product, 0.0)
@@ -90,6 +100,141 @@
 
     correction = smooth_twice(residual, diag_inv, apply_operator)
     return correction
+
+
+MESH = pl.DeviceIdType.MESH
+
+
+def smoother_kernel(
+    leads, members, slot_ref, cols_ref, tiles_ref, rhs_ref, inv_ref, out_ref,
+    mine, ext0, ext1, ext2, local_sem, tile_send, tile_recv, send_sem, recv_sem,
+):
+    lead, me = lax.axis_index("lead"), lax.axis_index("grp")
+    exts = (ext0, ext1, ext2)
+    share_tiles, tile_size, _ = tiles_ref.shape
+    rows, width = rhs_ref.shape
+    total_tiles = share_tiles * members
+    lower, upper = lax.rem(lead + leads - 1, leads), lax.rem(lead + 1, leads)
+    others = [lax.rem(me + i, members) for i in range(1, members)]
+    everyone = [me] + others
+
+    partners = [(lead, p) for p in others]
+    partners += [(lower, p) for p in everyone] + [(upper, p) for p in everyone]
+    barrier = pltpu.get_barrier_semaphore()
+    for partner in partners:
+        pl.semaphore_signal(barrier, inc=1, device_id=partner, device_id_type=MESH)
+
+    def rows_of(member):
+        return pl.ds(pl.multiple_of(member * rows, rows), rows)
+
+    def pieces(ext, block):
+        return ext.at[block] if block else ext.at[0, pl.ds(0, (members - 1) * rows)]
+
+    landing = mine.at[pl.ds(me * share_tiles, share_tiles)]
+    own_copy = pltpu.make_async_copy(tiles_ref.at[:, rows_of(me), :], landing, local_sem)
+    own_copy.start()
+
+    row_id = lax.broadcasted_iota(jnp.int32, (rows, rows), 0)
+    col_id = lax.broadcasted_iota(jnp.int32, (rows, rows), 1)
+    inverse = jnp.broadcast_to(inv_ref[...], (rows, rows))
+    inverse = jnp.sum(jnp.where(row_id == col_id, inverse, 0.0), axis=1, keepdims=True)
+    rhs = rhs_ref[...]
+    columns = [cols_ref[0, lax.rem(slot_ref[0, t], TILES_ROW)] for t in range(total_tiles)]
+
+    def push(step, field):
+        ext = exts[step]
+        here = ext.at[0, rows_of(me), :]
+        here[...] = field.astype(jnp.bfloat16)
+        if step == 0:
+            pl.semaphore_wait(barrier, len(partners))
+            for p in others:
+                pltpu.make_async_remote_copy(
+                    src_ref=tiles_ref.at[:, rows_of(p), :], dst_ref=landing,
+                    send_sem=tile_send, recv_sem=tile_recv,
+                    device_id=(lead, p), device_id_type=MESH,
+                ).start()
+        for block, to_lead, targets in ((1, upper, everyone), (2, lower, everyone), (0, lead, others)):
+            for p in targets:
+                pltpu.make_async_remote_copy(
+                    src_ref=here, dst_ref=ext.at[block, rows_of(me), :],
+                    send_sem=send_sem.at[step, block], recv_sem=recv_sem.at[step, block],
+                    device_id=(to_lead, p), device_id_type=MESH,
+                ).start()
+
+    def wait_for(ref, sem):
+        pltpu.make_async_copy(ref, ref, sem).wait()
+
+    def coupled(step):
+        ext = exts[step]
+        for block in range(3):
+            wait_for(pieces(ext, block), recv_sem.at[step, block])
+        if step == 0:
+            own_copy.wait()
+            wait_for(mine.at[pl.ds(0, (members - 1) * share_tiles)], tile_recv)
+        left = jnp.concatenate([mine[t] for t in range(total_tiles)], axis=1)
+        right = jnp.concatenate([ext[columns[t]] for t in range(total_tiles)], axis=0)
+        return jnp.dot(left, right, preferred_element_type=jnp.float32)
+
+    center = (upper_bound + lower_bound) / 2.0
+    half = (upper_bound - lower_bound) / 2.0
+    sigma = center / half
+    rho = 1.0 / sigma
+    rho_next = 1.0 / (2.0 * sigma - rho)
+    keep, gain = 1.0 + rho_next * rho, 2.0 * rho_next / half
+    rest = 1.0 - 1.0 / center
+
+    def sweep(step, start):
+        push(step, inverse * (start * (1.0 / center)))
+        product = coupled(step)
+        scaled = keep / center * start + gain * (rest * start - product)
+        return inverse * scaled, scaled
+
+    first, first_scaled = sweep(0, rhs)
+    push(1, first)
+    remaining = rhs - (first_scaled + coupled(1))
+    second, _ = sweep(2, remaining)
+    out_ref[...] = first + second
+
+    wait_for(tiles_ref.at[:, pl.ds(0, (members - 1) * rows), :], tile_send)
+    for step in range(3):
+        for block in range(3):
+            wait_for(pieces(exts[step], block), send_sem.at[step, block])
+
+
+def local_kernel(leads, members, matrix_tiles, tile_slot, tile_cols, send_rows, residual, diag_inv):
+    share_tiles, tile_size, _ = matrix_tiles.shape
+    rows, width = residual.shape
+    smem = pl.BlockSpec(memory_space=pltpu.SMEM)
+    vmem = pl.BlockSpec(memory_space=pltpu.VMEM)
+    work = 3 * 2 * rows * share_tiles * members * tile_size * width
+    return pl.pallas_call(
+        functools.partial(smoother_kernel, leads, members),
+        out_shape=jax.ShapeDtypeStruct(residual.shape, residual.dtype),
+        in_specs=[smem, smem, pl.BlockSpec(memory_space=pl.ANY), vmem, vmem],
+        out_specs=vmem,
+        scratch_shapes=[
+            pltpu.VMEM((members * share_tiles, rows, tile_size), jnp.bfloat16),
+            *[pltpu.VMEM((3, tile_size, width), jnp.bfloat16)] * 3,
+            pltpu.SemaphoreType.DMA,
+            pltpu.SemaphoreType.DMA,
+            pltpu.SemaphoreType.DMA,
+            pltpu.SemaphoreType.DMA((3, 3)),
+            pltpu.SemaphoreType.DMA((3, 3)),
+        ],
+        cost_estimate=pl.CostEstimate(
+            flops=work, bytes_accessed=matrix_tiles.size * 2 + residual.size * 8, transcendentals=0
+        ),
+        compiler_params=pltpu.CompilerParams(
+            collective_id=0, has_side_effects=True, vmem_limit_bytes=24 * 1024 * 1024
+        ),
+    )(tile_slot, tile_cols, matrix_tiles, residual, diag_inv.reshape(1, rows))
+
+
+def local(*args):
+    leads, members = lax.axis_size("lead"), lax.axis_size("grp")
+    if args[2].shape[0] == 1 and leads > 2 and members > 1:
+        return local_kernel(leads, members, *args)
+    return local_general(*args)
 
 
 def solution(mesh):

time: 70.4 us -> 32 us (0.45)
  Pallas kernels: 0 us -> 28.6 us
  blocking collectives: 25.5 us -> 0 us
  starting transfers between devices: 14.4 us -> 0 us
  waiting for transfers between devices: 11.3 us -> 0 us
  local copies, waits for them, and re-layouts: 9.34 us -> 3.17 us
  between operations: 4.27 us -> 0.01 us
  other arithmetic: 3.06 us -> 0 us
  matrix products: 2.11 us -> 0 us
    pallas_call x0 -> x1, Pallas kernels: none -> 28.6 us  [local_kernel(): pl.pallas_call(functools.partial(smoother_kernel, leads, members), out_sh...]
    all_gather x3 -> x0, blocking collectives: 25.5 us -> none  [apply_operator(): gathered = lax.all_gather(rounded, 'grp', axis=0, tiled=True)]
    ppermute x6 -> x0, starting transfers between devices: 10.8 us -> none  [from_behind(): lax.ppermute(shard, axis, [(i, (i + by) % devices) for i in range(devices)])]
    gather x4 -> x0, local copies, waits for them, and re-layouts: 7.17 us -> none  [the longest x1 5.07 us: local(): picked = matrix_tiles[tile_pick, clipped]]
    all_to_all x1 -> x0, waiting for transfers between devices: 6.4 us -> none  [local(): lax.all_to_all(outgoing, 'grp', split_axis=0, concat_axis=0, tiled=True)]
    ppermute x6 -> x0, waiting for transfers between devices: 4.93 us -> none  [from_behind(): lax.ppermute(shard, axis, [(i, (i + by) % devices) for i in range(devices)])]
    all_to_all x1 -> x0, starting transfers between devices: 3.61 us -> none  [local(): lax.all_to_all(outgoing, 'grp', split_axis=0, concat_axis=0, tiled=True)]
    unnamed x11, local copies, waits for them, and re-layouts: 0.69 us -> 3.17 us
  transfers between devices with their start and end apart: 7 -> 0, of which waited for: 3 -> 0; matrix products, arithmetic and copies ran while one was open for 11% -> 0% of each run, Pallas kernels for 0% -> 0%
where the time goes in v1:
time: 32 us; the launch traced here: 31.8 us
  Pallas kernels  28.6 us (89%)
  local copies, waits for them, and re-layouts  3.17 us (10%)
    pallas_call x1, Pallas kernels, local_kernel(): pl.pallas_call(functools.partial(smoother_kernel, leads, members), out_sh...  28.6 us
    unnamed x11, local copies, waits for them, and re-layouts  3.17 us

profile of v1, /device:TPU:0, one launch (start us, length us, event | category | flops | bytes accessed | tf_op | source)
XLA Modules:
  0.0 31.8 jit_solution(10821579521825095566)
XLA Ops:
  0.0 0.0 copy-start.4
  0.0 0.0 copy-start.3
  0.0 0.0 copy-start.2
  0.0 0.6 %copy-done.4 = f32[96]{0:T(128)S(1)} copy-done((f32[96]{0:T(128)S(1)}, f32[96]{0:T(128)}, u32[]{:S(2)}) %copy-start.4) | copy-done | bytes 408
  0.7 0.0 copy-done.3
  0.7 0.0 copy-done.2
  0.7 0.0 copy-start
  0.7 1.1 %copy-done = bf16[2,384,384]{2,1,0:T(8,128)(2,1)S(1)} copy-done((bf16[2,384,384]{2,1,0:T(8,128)(2,1)S(1)}, bf16[2,384,384]{2,1,0:T(8,128)(2,1)}, u32[]{:S(2)}) %copy-start) | copy-done | bytes 589848
  1.8 0.0 copy-start.1
  1.8 0.8 %copy-done.1 = f32[96,128]{1,0:T(8,128)S(1)} copy-done((f32[96,128]{1,0:T(8,128)S(1)}, f32[96,128]{1,0:T(8,128)}, u32[]{:S(2)}) %copy-start.1) | copy-done | bytes 49176
  2.6 28.6 %shard_map.55 = f32[96,128]{1,0:T(8,128)S(1)} custom-call(s32[1,8]{1,0:T(1,128)S(1)} %copy-done.2, s32[1,8]{1,0:T(1,128)S(1)} %copy-done.3, bf16[2,384,384]{2,1,0:T(8,128)(2,1)S(1)} %copy-done, f32[96,128]{1,0:T(8,128)S(1)} %copy-done.1, f32[1,96]{1,0:T(1,128)S(1)} %bitcast.1), custom_call_target="tpu_custom_call" | custom-call | flops 226492416 | bytes 688128 | tf_op jit(solution)/shard_map/pallas_call | solution.py:210
  31.2 0.6 %copy.7 = f32[96,128]{1,0:T(8,128)} copy(f32[96,128]{1,0:T(8,128)S(1)} %shard_map.55) | data formatting | bytes 98304
Async XLA Ops:
  0.0 0.7 %copy-start.4 = (f32[96]{0:T(128)S(1)}, f32[96]{0:T(128)}, u32[]{:S(2)}) copy-start(f32[96]{0:T(128)} %param.10) | copy-start | bytes 1156
  0.0 0.7 %copy-start.3 = (s32[1,8]{1,0:T(1,128)S(1)}, s32[1,8]{1,0:T(1,128)}, u32[]{:S(2)}) copy-start(s32[1,8]{1,0:T(1,128)} %cols_ref.1) | copy-start | bytes 100
  0.0 0.7 %copy-start.2 = (s32[1,8]{1,0:T(1,128)S(1)}, s32[1,8]{1,0:T(1,128)}, u32[]{:S(2)}) copy-start(s32[1,8]{1,0:T(1,128)} %slot_ref.1) | copy-start | bytes 100
  0.7 1.1 %copy-start = (bf16[2,384,384]{2,1,0:T(8,128)(2,1)S(1)}, bf16[2,384,384]{2,1,0:T(8,128)(2,1)}, u32[]{:S(2)}) copy-start(bf16[2,384,384]{2,1,0:T(8,128)(2,1)} %tiles_ref.1) | copy-start | bytes 1769476
  1.8 0.8 %copy-start.1 = (f32[96,128]{1,0:T(8,128)S(1)}, f32[96,128]{1,0:T(8,128)}, u32[]{:S(2)}) copy-start(f32[96,128]{1,0:T(8,128)} %rhs_ref.1) | copy-start | bytes 147460

commit v2 on v1

--- a/solution.py
+++ b/solution.py
@@ -106,13 +106,13 @@
 
 
 def smoother_kernel(
-    leads, members, slot_ref, cols_ref, tiles_ref, rhs_ref, inv_ref, out_ref,
-    mine, ext0, ext1, ext2, local_sem, tile_send, tile_recv, send_sem, recv_sem,
+    leads, members, slot_ref, cols_ref, tiles_ref, rhs_in, inv_in, out_ref,
+    rhs_ref, inv_ref, mine, ext0, ext1, ext2, local_sem, tile_send, tile_recv, send_sem, recv_sem,
 ):
     lead, me = lax.axis_index("lead"), lax.axis_index("grp")
     exts = (ext0, ext1, ext2)
     share_tiles, tile_size, _ = tiles_ref.shape
-    rows, width = rhs_ref.shape
+    rows, width = rhs_in.shape
     total_tiles = share_tiles * members
     lower, upper = lax.rem(lead + leads - 1, leads), lax.rem(lead + 1, leads)
     others = [lax.rem(me + i, members) for i in range(1, members)]
@@ -131,28 +131,34 @@
         return ext.at[block] if block else ext.at[0, pl.ds(0, (members - 1) * rows)]
 
     landing = mine.at[pl.ds(me * share_tiles, share_tiles)]
-    own_copy = pltpu.make_async_copy(tiles_ref.at[:, rows_of(me), :], landing, local_sem)
+    load_rhs = pltpu.make_async_copy(rhs_in, rhs_ref, local_sem.at[0])
+    load_rhs.start()
+    load_inv = pltpu.make_async_copy(inv_in, inv_ref, local_sem.at[1])
+    load_inv.start()
+    own_copy = pltpu.make_async_copy(tiles_ref.at[:, rows_of(me), :], landing, local_sem.at[2])
     own_copy.start()
+    columns = [cols_ref[0, lax.rem(slot_ref[0, t], TILES_ROW)] for t in range(total_tiles)]
+
+    pl.semaphore_wait(barrier, len(partners))
+    for p in others:
+        pltpu.make_async_remote_copy(
+            src_ref=tiles_ref.at[:, rows_of(p), :], dst_ref=landing,
+            send_sem=tile_send, recv_sem=tile_recv,
+            device_id=(lead, p), device_id_type=MESH,
+        ).start()
+    load_rhs.wait()
+    load_inv.wait()
 
     row_id = lax.broadcasted_iota(jnp.int32, (rows, rows), 0)
     col_id = lax.broadcasted_iota(jnp.int32, (rows, rows), 1)
     inverse = jnp.broadcast_to(inv_ref[...], (rows, rows))
     inverse = jnp.sum(jnp.where(row_id == col_id, inverse, 0.0), axis=1, keepdims=True)
     rhs = rhs_ref[...]
-    columns = [cols_ref[0, lax.rem(slot_ref[0, t], TILES_ROW)] for t in range(total_tiles)]
 
     def push(step, field):
         ext = exts[step]
         here = ext.at[0, rows_of(me), :]
         here[...] = field.astype(jnp.bfloat16)
-        if step == 0:
-            pl.semaphore_wait(barrier, len(partners))
-            for p in others:
-                pltpu.make_async_remote_copy(
-                    src_ref=tiles_ref.at[:, rows_of(p), :], dst_ref=landing,
-                    send_sem=tile_send, recv_sem=tile_recv,
-                    device_id=(lead, p), device_id_type=MESH,
-                ).start()
         for block, to_lead, targets in ((1, upper, everyone), (2, lower, everyone), (0, lead, others)):
             for p in targets:
                 pltpu.make_async_remote_copy(
@@ -206,16 +212,19 @@
     rows, width = residual.shape
     smem = pl.BlockSpec(memory_space=pltpu.SMEM)
     vmem = pl.BlockSpec(memory_space=pltpu.VMEM)
+    anywhere = pl.BlockSpec(memory_space=pl.ANY)
     work = 3 * 2 * rows * share_tiles * members * tile_size * width
     return pl.pallas_call(
         functools.partial(smoother_kernel, leads, members),
         out_shape=jax.ShapeDtypeStruct(residual.shape, residual.dtype),
-        in_specs=[smem, smem, pl.BlockSpec(memory_space=pl.ANY), vmem, vmem],
+        in_specs=[smem, smem, anywhere, anywhere, anywhere],
         out_specs=vmem,
         scratch_shapes=[
+            pltpu.VMEM((rows, width), residual.dtype),
+            pltpu.VMEM((1, rows), diag_inv.dtype),
             pltpu.VMEM((members * share_tiles, rows, tile_size), jnp.bfloat16),
             *[pltpu.VMEM((3, tile_size, width), jnp.bfloat16)] * 3,
-            pltpu.SemaphoreType.DMA,
+            pltpu.SemaphoreType.DMA((3,)),
             pltpu.SemaphoreType.DMA,
             pltpu.SemaphoreType.DMA,
             pltpu.SemaphoreType.DMA((3, 3)),
@@ -225,7 +234,7 @@
             flops=work, bytes_accessed=matrix_tiles.size * 2 + residual.size * 8, transcendentals=0
         ),
         compiler_params=pltpu.CompilerParams(
-            collective_id=0, has_side_effects=True, vmem_limit_bytes=24 * 1024 * 1024
+            collective_id=0, has_side_effects=True, vmem_limit_bytes=60 * 1024 * 1024
         ),
     )(tile_slot, tile_cols, matrix_tiles, residual, diag_inv.reshape(1, rows))
 

time: 32 us -> 31.2 us (0.975)
  local copies, waits for them, and re-layouts: 3.17 us -> 1.42 us
  Pallas kernels: 28.6 us -> 29.6 us
    unnamed x11 -> x1, local copies, waits for them, and re-layouts: 3.17 us -> 1.42 us
    pallas_call x1, Pallas kernels: 28.6 us -> 29.6 us  [local_kernel(): pl.pallas_call(functools.partial(smoother_kernel, leads, members), out_sh...]
where the time goes in v2:
time: 31.2 us; the launch traced here: 31 us
  Pallas kernels  29.6 us (95%)
  local copies, waits for them, and re-layouts  1.42 us (5%)
    pallas_call x1, Pallas kernels, local_kernel(): pl.pallas_call(functools.partial(smoother_kernel, leads, members), out_sh...  29.6 us
    unnamed x1, local copies, waits for them, and re-layouts  1.42 us

profile of v2, /device:TPU:0, one launch (start us, length us, event | category | flops | bytes accessed | tf_op | source)
XLA Modules:
  0.0 31.0 jit_solution(15082263105157127048)
XLA Ops:
  0.0 29.6 %shard_map.55 = f32[96,128]{1,0:T(8,128)} custom-call(s32[1,8]{1,0:T(1,128)} %slot_ref.1, s32[1,8]{1,0:T(1,128)} %cols_ref.1, bf16[2,384,384]{2,1,0:T(8,128)(2,1)} %tiles_ref.1, f32[96,128]{1,0:T(8,128)} %rhs_in.1, f32[1,96]{1,0:T(1,128)} %bitcast.1), custom_call_target="tpu_custom_call" | custom-call | flops 226492416 | bytes 688128 | tf_op jit(solution)/shard_map/pallas_call | solution.py:217
  29.6 1.4 %copy.7 = f32[96,128]{1,0:T(8,128)} copy(f32[96,128]{1,0:T(8,128)} %shard_map.55) | data formatting | bytes 98304

commit v3 on v2

--- a/solution.py
+++ b/solution.py
@@ -212,7 +212,7 @@
     rows, width = residual.shape
     smem = pl.BlockSpec(memory_space=pltpu.SMEM)
     vmem = pl.BlockSpec(memory_space=pltpu.VMEM)
-    anywhere = pl.BlockSpec(memory_space=pl.ANY)
+    anywhere = pl.BlockSpec(memory_space=pltpu.HBM)
     work = 3 * 2 * rows * share_tiles * members * tile_size * width
     return pl.pallas_call(
         functools.partial(smoother_kernel, leads, members),
@@ -234,7 +234,7 @@
             flops=work, bytes_accessed=matrix_tiles.size * 2 + residual.size * 8, transcendentals=0
         ),
         compiler_params=pltpu.CompilerParams(
-            collective_id=0, has_side_effects=True, vmem_limit_bytes=60 * 1024 * 1024
+            collective_id=0, has_side_effects=True, vmem_limit_bytes=24 * 1024 * 1024
         ),
     )(tile_slot, tile_cols, matrix_tiles, residual, diag_inv.reshape(1, rows))
 

time: 31.2 us -> 32 us (1.026)
  local copies, waits for them, and re-layouts: 1.42 us -> 3.17 us
  Pallas kernels: 29.6 us -> 28.6 us
    unnamed x1 -> x11, local copies, waits for them, and re-layouts: 1.42 us -> 3.17 us
    pallas_call x1, Pallas kernels: 29.6 us -> 28.6 us  [local_kernel(): pl.pallas_call(functools.partial(smoother_kernel, leads, members), out_sh...]
where the time goes in v3:
time: 32 us; the launch traced here: 31.8 us
  Pallas kernels  28.6 us (89%)
  local copies, waits for them, and re-layouts  3.17 us (10%)
    pallas_call x1, Pallas kernels, local_kernel(): pl.pallas_call(functools.partial(smoother_kernel, leads, members), out_sh...  28.6 us
    unnamed x11, local copies, waits for them, and re-layouts  3.17 us

profile of v3, /device:TPU:0, one launch (start us, length us, event | category | flops | bytes accessed | tf_op | source)
XLA Modules:
  0.0 31.8 jit_solution(5722159887536391746)
XLA Ops:
  0.0 0.0 copy-start.4
  0.0 0.0 copy-start.3
  0.0 0.0 copy-start.2
  0.0 0.6 %copy-done.4 = f32[96]{0:T(128)S(1)} copy-done((f32[96]{0:T(128)S(1)}, f32[96]{0:T(128)}, u32[]{:S(2)}) %copy-start.4) | copy-done | bytes 408
  0.7 0.0 copy-done.3
  0.7 0.0 copy-done.2
  0.7 0.0 copy-start
  0.7 1.1 %copy-done = bf16[2,384,384]{2,1,0:T(8,128)(2,1)S(1)} copy-done((bf16[2,384,384]{2,1,0:T(8,128)(2,1)S(1)}, bf16[2,384,384]{2,1,0:T(8,128)(2,1)}, u32[]{:S(2)}) %copy-start) | copy-done | bytes 589848
  1.8 0.0 copy-start.1
  1.8 0.8 %copy-done.1 = f32[96,128]{1,0:T(8,128)S(1)} copy-done((f32[96,128]{1,0:T(8,128)S(1)}, f32[96,128]{1,0:T(8,128)}, u32[]{:S(2)}) %copy-start.1) | copy-done | bytes 49176
  2.6 28.6 %shard_map.55 = f32[96,128]{1,0:T(8,128)S(1)} custom-call(s32[1,8]{1,0:T(1,128)S(1)} %copy-done.2, s32[1,8]{1,0:T(1,128)S(1)} %copy-done.3, bf16[2,384,384]{2,1,0:T(8,128)(2,1)S(1)} %copy-done, f32[96,128]{1,0:T(8,128)S(1)} %copy-done.1, f32[1,96]{1,0:T(1,128)S(1)} %bitcast.1), custom_call_target="tpu_custom_call" | custom-call | flops 226492416 | bytes 688128 | tf_op jit(solution)/shard_map/pallas_call | solution.py:217
  31.2 0.6 %copy.7 = f32[96,128]{1,0:T(8,128)} copy(f32[96,128]{1,0:T(8,128)S(1)} %shard_map.55) | data formatting | bytes 98304
Async XLA Ops:
  0.0 0.7 %copy-start.4 = (f32[96]{0:T(128)S(1)}, f32[96]{0:T(128)}, u32[]{:S(2)}) copy-start(f32[96]{0:T(128)} %param.10) | copy-start | bytes 1156
  0.0 0.7 %copy-start.3 = (s32[1,8]{1,0:T(1,128)S(1)}, s32[1,8]{1,0:T(1,128)}, u32[]{:S(2)}) copy-start(s32[1,8]{1,0:T(1,128)} %cols_ref.1) | copy-start | bytes 100
  0.0 0.7 %copy-start.2 = (s32[1,8]{1,0:T(1,128)S(1)}, s32[1,8]{1,0:T(1,128)}, u32[]{:S(2)}) copy-start(s32[1,8]{1,0:T(1,128)} %slot_ref.1) | copy-start | bytes 100
  0.7 1.1 %copy-start = (bf16[2,384,384]{2,1,0:T(8,128)(2,1)S(1)}, bf16[2,384,384]{2,1,0:T(8,128)(2,1)}, u32[]{:S(2)}) copy-start(bf16[2,384,384]{2,1,0:T(8,128)(2,1)} %tiles_ref.1) | copy-start | bytes 1769476
  1.8 0.8 %copy-start.1 = (f32[96,128]{1,0:T(8,128)S(1)}, f32[96,128]{1,0:T(8,128)}, u32[]{:S(2)}) copy-start(f32[96,128]{1,0:T(8,128)} %rhs_in.1) | copy-start | bytes 147460

commit v4 on v2

--- a/solution.py
+++ b/solution.py
@@ -107,19 +107,22 @@
 
 def smoother_kernel(
     leads, members, slot_ref, cols_ref, tiles_ref, rhs_in, inv_in, out_ref,
-    rhs_ref, inv_ref, mine, ext0, ext1, ext2, local_sem, tile_send, tile_recv, send_sem, recv_sem,
+    rhs_ref, inv_ref, mine, ext0, ext1, ext2, local_sem, tile_send, tile_recv, send_sem, recv_sem, group_sem,
 ):
     lead, me = lax.axis_index("lead"), lax.axis_index("grp")
     exts = (ext0, ext1, ext2)
     share_tiles, tile_size, _ = tiles_ref.shape
     rows, width = rhs_in.shape
     total_tiles = share_tiles * members
-    lower, upper = lax.rem(lead + leads - 1, leads), lax.rem(lead + 1, leads)
+    odd = lax.rem(lead, 2)
+    mate = lead + 1 - 2 * odd
+    far = lax.rem(lead + leads - 1 + 2 * odd, leads)
+    at_mate, at_far = 1 + odd, 2 - odd
     others = [lax.rem(me + i, members) for i in range(1, members)]
     everyone = [me] + others
 
     partners = [(lead, p) for p in others]
-    partners += [(lower, p) for p in everyone] + [(upper, p) for p in everyone]
+    partners += [(far, p) for p in everyone] + [(mate, me)]
     barrier = pltpu.get_barrier_semaphore()
     for partner in partners:
         pl.semaphore_signal(barrier, inc=1, device_id=partner, device_id_type=MESH)
@@ -139,13 +142,6 @@
     own_copy.start()
     columns = [cols_ref[0, lax.rem(slot_ref[0, t], TILES_ROW)] for t in range(total_tiles)]
 
-    pl.semaphore_wait(barrier, len(partners))
-    for p in others:
-        pltpu.make_async_remote_copy(
-            src_ref=tiles_ref.at[:, rows_of(p), :], dst_ref=landing,
-            send_sem=tile_send, recv_sem=tile_recv,
-            device_id=(lead, p), device_id_type=MESH,
-        ).start()
     load_rhs.wait()
     load_inv.wait()
 
@@ -159,21 +155,48 @@
         ext = exts[step]
         here = ext.at[0, rows_of(me), :]
         here[...] = field.astype(jnp.bfloat16)
-        for block, to_lead, targets in ((1, upper, everyone), (2, lower, everyone), (0, lead, others)):
-            for p in targets:
+        if step == 0:
+            pl.semaphore_wait(barrier, len(partners))
+        for i, p in enumerate(others):
+            pltpu.make_async_remote_copy(
+                src_ref=here, dst_ref=here,
+                send_sem=send_sem.at[step, 0], recv_sem=group_sem.at[step, i],
+                device_id=(lead, p), device_id_type=MESH,
+            ).start()
+        for p in everyone:
+            pltpu.make_async_remote_copy(
+                src_ref=here, dst_ref=ext.at[at_far, rows_of(me), :],
+                send_sem=send_sem.at[step, 1], recv_sem=recv_sem.at[step, at_far],
+                device_id=(far, p), device_id_type=MESH,
+            ).start()
+        pass_on(step, me)
+        if step == 0:
+            for p in others:
                 pltpu.make_async_remote_copy(
-                    src_ref=here, dst_ref=ext.at[block, rows_of(me), :],
-                    send_sem=send_sem.at[step, block], recv_sem=recv_sem.at[step, block],
-                    device_id=(to_lead, p), device_id_type=MESH,
+                    src_ref=tiles_ref.at[:, rows_of(p), :], dst_ref=landing,
+                    send_sem=tile_send, recv_sem=tile_recv,
+                    device_id=(lead, p), device_id_type=MESH,
                 ).start()
+
+    def pass_on(step, owner):
+        ext = exts[step]
+        pltpu.make_async_remote_copy(
+            src_ref=ext.at[0, rows_of(owner), :], dst_ref=ext.at[at_mate, rows_of(owner), :],
+            send_sem=send_sem.at[step, 2], recv_sem=recv_sem.at[step, at_mate],
+            device_id=(mate, me), device_id_type=MESH,
+        ).start()
 
     def wait_for(ref, sem):
         pltpu.make_async_copy(ref, ref, sem).wait()
 
     def coupled(step):
         ext = exts[step]
-        for block in range(3):
-            wait_for(pieces(ext, block), recv_sem.at[step, block])
+        for i in range(1, members):
+            owner = lax.rem(me + members - i, members)
+            wait_for(ext.at[0, rows_of(owner), :], group_sem.at[step, i - 1])
+            pass_on(step, owner)
+        for block in (1, 2):
+            wait_for(ext.at[block], recv_sem.at[step, block])
         if step == 0:
             own_copy.wait()
             wait_for(mine.at[pl.ds(0, (members - 1) * share_tiles)], tile_recv)
@@ -229,6 +252,7 @@
             pltpu.SemaphoreType.DMA,
             pltpu.SemaphoreType.DMA((3, 3)),
             pltpu.SemaphoreType.DMA((3, 3)),
+            pltpu.SemaphoreType.DMA((3, members - 1)),
         ],
         cost_estimate=pl.CostEstimate(
             flops=work, bytes_accessed=matrix_tiles.size * 2 + residual.size * 8, transcendentals=0
@@ -241,7 +265,7 @@
 
 def local(*args):
     leads, members = lax.axis_size("lead"), lax.axis_size("grp")
-    if args[2].shape[0] == 1 and leads > 2 and members > 1:
+    if args[2].shape[0] == 1 and leads > 2 and leads % 2 == 0 and members > 1:
         return local_kernel(leads, members, *args)
     return local_general(*args)
 

time: 31.2 us -> 30 us (0.962)
  Pallas kernels: 29.6 us -> 28.4 us
    pallas_call x1, Pallas kernels: 29.6 us -> 28.4 us  [local_kernel(): pl.pallas_call(functools.partial(smoother_kernel, leads, members), out_sh...]
where the time goes in v4:
time: 30 us; the launch traced here: 29.8 us
  Pallas kernels  28.4 us (95%)
  local copies, waits for them, and re-layouts  1.42 us (5%)
    pallas_call x1, Pallas kernels, local_kernel(): pl.pallas_call(functools.partial(smoother_kernel, leads, members), out_sh...  28.4 us
    unnamed x1, local copies, waits for them, and re-layouts  1.42 us

profile of v4, /device:TPU:0, one launch (start us, length us, event | category | flops | bytes accessed | tf_op | source)
XLA Modules:
  0.0 29.8 jit_solution(18229388208646917622)
XLA Ops:
  0.0 28.4 %shard_map.55 = f32[96,128]{1,0:T(8,128)} custom-call(s32[1,8]{1,0:T(1,128)} %slot_ref.1, s32[1,8]{1,0:T(1,128)} %cols_ref.1, bf16[2,384,384]{2,1,0:T(8,128)(2,1)} %tiles_ref.1, f32[96,128]{1,0:T(8,128)} %rhs_in.1, f32[1,96]{1,0:T(1,128)} %bitcast.1), custom_call_target="tpu_custom_call" | custom-call | flops 226492416 | bytes 688128 | tf_op jit(solution)/shard_map/pallas_call | solution.py:240
  28.4 1.4 %copy.7 = f32[96,128]{1,0:T(8,128)} copy(f32[96,128]{1,0:T(8,128)} %shard_map.55) | data formatting | bytes 98304

commit v5 on v4

--- a/solution.py
+++ b/solution.py
@@ -258,7 +258,7 @@
             flops=work, bytes_accessed=matrix_tiles.size * 2 + residual.size * 8, transcendentals=0
         ),
         compiler_params=pltpu.CompilerParams(
-            collective_id=0, has_side_effects=True, vmem_limit_bytes=60 * 1024 * 1024
+            collective_id=0, has_side_effects=True, vmem_limit_bytes=55168 * 1024
         ),
     )(tile_slot, tile_cols, matrix_tiles, residual, diag_inv.reshape(1, rows))
 

time: 30 us -> 29.1 us (0.970)
  Pallas kernels: 28.4 us -> 27.7 us
    pallas_call x1, Pallas kernels: 28.4 us -> 27.7 us  [local_kernel(): pl.pallas_call(functools.partial(smoother_kernel, leads, members), out_sh...]
    unnamed x1 -> x7, local copies, waits for them, and re-layouts: 1.42 us -> 1.31 us
where the time goes in v5:
time: 29.1 us; the launch traced here: 29 us
  Pallas kernels  27.7 us (95%)
  local copies, waits for them, and re-layouts  1.31 us (5%)
    pallas_call x1, Pallas kernels, local_kernel(): pl.pallas_call(functools.partial(smoother_kernel, leads, members), out_sh...  27.7 us
    unnamed x7, local copies, waits for them, and re-layouts  1.31 us

profile of v5, /device:TPU:0, one launch (start us, length us, event | category | flops | bytes accessed | tf_op | source)
XLA Modules:
  0.0 29.0 jit_solution(18414185346975887093)
XLA Ops:
  0.0 0.0 copy-start.2
  0.0 0.0 copy-start.1
  0.0 0.0 copy-start
  0.0 0.6 %copy-done.2 = f32[96]{0:T(128)S(1)} copy-done((f32[96]{0:T(128)S(1)}, f32[96]{0:T(128)}, u32[]{:S(2)}) %copy-start.2) | copy-done | bytes 408
  0.7 0.0 copy-done.1
  0.7 0.0 copy-done
  0.7 27.7 %shard_map.55 = f32[96,128]{1,0:T(8,128)S(1)} custom-call(s32[1,8]{1,0:T(1,128)S(1)} %copy-done, s32[1,8]{1,0:T(1,128)S(1)} %copy-done.1, bf16[2,384,384]{2,1,0:T(8,128)(2,1)} %tiles_ref.1, f32[96,128]{1,0:T(8,128)} %rhs_in.1, f32[1,96]{1,0:T(1,128)S(1)} %bitcast.1), custom_call_target="tpu_custom_call" | custom-call | flops 226492416 | bytes 688128 | tf_op jit(solution)/shard_map/pallas_call | solution.py:240
  28.3 0.6 %copy.7 = f32[96,128]{1,0:T(8,128)} copy(f32[96,128]{1,0:T(8,128)S(1)} %shard_map.55) | data formatting | bytes 98304
Async XLA Ops:
  0.0 0.7 %copy-start.2 = (f32[96]{0:T(128)S(1)}, f32[96]{0:T(128)}, u32[]{:S(2)}) copy-start(f32[96]{0:T(128)} %param.10) | copy-start | bytes 1156
  0.0 0.7 %copy-start.1 = (s32[1,8]{1,0:T(1,128)S(1)}, s32[1,8]{1,0:T(1,128)}, u32[]{:S(2)}) copy-start(s32[1,8]{1,0:T(1,128)} %cols_ref.1) | copy-start | bytes 100
  0.0 0.7 %copy-start = (s32[1,8]{1,0:T(1,128)S(1)}, s32[1,8]{1,0:T(1,128)}, u32[]{:S(2)}) copy-start(s32[1,8]{1,0:T(1,128)} %slot_ref.1) | copy-start | bytes 100
